TPU v7x, 512 devices: a whole 4x4x16 slice. The times are simulated.
512 devices in a mesh: dp: 32 (over z, x_hi), mrow: 8 (over y, x_lo), mcol: 2 (over core).
Axes of the slice: x: 4 (x_hi: 2, x_lo: 2; x = x_hi * 2 + x_lo), y: 4, z: 16, core: 2. Of those that a mesh axis runs over, the one named last changes fastest.
Arguments:
- inputs: bfloat16 [32768, 8192], P('dp', 'mrow'), may hold values from -6 to 6
- kv_grads: bfloat16 [32768, 512], P('dp', 'mcol'), may hold values from -6 to 6
- weight: bfloat16 [8192, 512], P('mrow', 'mcol'), may hold values from -0.25 to 0.25
- master: float32 [8, 32, 32, 512], P('mrow', 'dp', None, 'mcol'), may hold values from -6 to 6
- row_state: float32 [2, 8, 32, 32], P('mcol', 'mrow', 'dp'), may hold values from 65.536 to 16384
- col_state: float32 [2, 256], P('mcol'), may hold values from 65.536 to 16384
Outputs:
- new_master: float32 [8, 32, 32, 512], P('mrow', 'dp', None, 'mcol')
- new_rows: float32 [2, 8, 32, 32], P('mcol', 'mrow', 'dp')
- new_cols: float32 [2, 256], P('mcol')
- new_weight: bfloat16 [8192, 512], P('mrow', 'mcol')
- input_grad: bfloat16 [32768, 8192], P('dp', ('mrow', 'mcol'))
All inputs are finite; a program needn't handle non-finite values.
Results may differ from a plain program's by a relative error of at most 0.0051.
Values may be sent and summed in bfloat16 or wider, within the bound.
A program may use at most 64 MiB of HBM per device.

v0:
```python
import jax
import jax.numpy as jnp
from jax import lax
from jax.sharding import PartitionSpec as P

D = 8192
HEAD = 256


def on_device(inputs, kv_grads, weight, master, row_state, col_state):
    grad = lax.psum_scatter(
        lax.dot_general(
            inputs, kv_grads, (((0,), (0,)), ((), ())), preferred_element_type=jnp.float32
        ),
        "dp",
        scatter_dimension=0,
        tiled=True,
    )
    term = jnp.dot(kv_grads, weight.T, preferred_element_type=jnp.float32)
    input_grad = lax.psum_scatter(
        term.astype(jnp.bfloat16), "mcol", scatter_dimension=1, tiled=True
    )
    params = master[0, 0]
    param_sq = jnp.sum(params * params)
    squared = grad * grad + 1e-30
    row_new = 0.8 * row_state[0, 0, 0] + 0.2 * jnp.mean(squared, axis=1)
    col_part = jnp.sum(squared, axis=0)
    row_total = jnp.sum(row_new)
    col_sum, row_sum, param_total = lax.psum((col_part, row_total, param_sq), ("dp", "mrow"))
    col_new = 0.8 * col_state[0] + 0.2 * col_sum / D
    row_avg = row_sum / D
    update = grad / jnp.sqrt(row_new[:, None] * col_new[None, :] / row_avg)
    update_sq = lax.psum(jnp.sum(update * update), ("dp", "mrow"))
    update_rms = jnp.sqrt(update_sq / (D * HEAD))
    param_rms = jnp.sqrt(param_total / (D * HEAD))
    clip = jnp.maximum(jnp.float32(1.0), update_rms)
    new_params = params - 0.5 * param_rms * update / clip
    new_weight = lax.all_gather(new_params.astype(jnp.bfloat16), "dp", axis=0, tiled=True)
    new_master = new_params[None, None]
    new_rows = row_new[None, None, None]
    new_cols = col_new[None]
    return (new_master, new_rows, new_cols, new_weight, input_grad)


def solution(mesh):
    placed = (
        P("dp", "mrow"),
        P("dp", "mcol"),
        P("mrow", "mcol"),
        P("mrow", "dp", None, "mcol"),
        P("mcol", "mrow", "dp", None),
        P("mcol", None),
    )
    return jax.shard_map(
        on_device,
        mesh=mesh,
        in_specs=placed,
        out_specs=(
            P("mrow", "dp", None, "mcol"),
            P("mcol", "mrow", "dp", None),
            P("mcol", None),
            P("mrow", "mcol"),
            P("dp", ("mrow", "mcol")),
        ),
        check_vma=False,
    )
```

profile of v0, /device:TPU:24, one launch (start us, length us, event | category | flops | bytes accessed | tf_op | source)
XLA Modules:
  0.0 2136.8 jit_solution(14553933474846188153)
XLA Ops:
  7.2 0.0 copy-start
  7.2 0.0 copy-start.1
  7.2 0.0 copy-start.2
  7.2 0.0 reduce-scatter.3.cloned.1.call-start
  7.2 1.5 copy-done
  8.8 2.8 fusion.5
  11.5 0.0 reduce-scatter.3.cloned.1.call-update
  11.6 0.0 copy-start.3
  11.6 0.0 copy-start.5
  11.6 0.0 copy-start.6
  11.6 0.0 reduce-scatter.5.cloned.1.call-start
  11.6 0.0 copy-done.1
  11.6 0.0 copy-done.2
  11.7 2.1 convolution_convert_fusion
  13.8 0.0 reduce-scatter.5.cloned.1.call-update
  13.8 0.0 copy-done.3
  13.8 0.6 fusion
  14.4 0.0 copy-done.5
  14.4 663.6 %reduce-scatter.3.cloned.1.call-done = f32[32,256]{1,0:T(8,128)} async-done(((f32[1024,256]{1,0:T(8,128)}), f32[32,256]{1,0:T(8,128)}) %reduce-scatter.3.cloned.1.call-update) | async-done | bytes 32784 | tf_op jit(solution)/shard_map/reduce_scatter | solution.py:11
  678.0 0.9 fusion.1
  678.9 0.0 copy-done.6
  678.9 0.6 fusion.4
  679.5 672.2 %all-reduce.1 = (f32[]{:T(128)}, f32[256]{0:T(256)S(1)}) all-reduce(f32[]{:T(128)} %get-tuple-element.13, f32[256]{0:T(256)S(1)} %get-tuple-element.5), channel_id=1, replica_groups=mesh['dp'=32,'mrow'=8,'mcol'=2] {'dp','mrow'}, use_global_device_ids=true, to_apply=%region_7.0 | all-reduce | flops 257 | bytes 2056 | tf_op jit(solution)/shard_map/psum | solution.py:29
  1352.4 0.0 copy-start.4
  1352.4 1.5 multiply_reduce_fusion
  1353.9 683.7 %all-reduce = (f32[]{:T(128)}, f32[]{:T(128)}) all-reduce(f32[]{:T(128)} %multiply_reduce_fusion, f32[]{:T(128)} %fusion), channel_id=1, replica_groups=mesh['dp'=32,'mrow'=8,'mcol'=2] {'dp','mrow'}, use_global_device_ids=true, to_apply=%region_9.0 | all-reduce | flops 2 | bytes 16 | tf_op jit(solution)/shard_map/psum | solution.py:33
  2039.0 1.5 fusion.3
  2040.5 88.2 %all_gather.3 = bf16[1024,256]{1,0:T(8,128)(2,1)S(1)} all-gather(bf16[32,256]{1,0:T(8,128)(2,1)S(1)} %get-tuple-element.11), channel_id=1, replica_groups=mesh['dp'=32,'mrow'=8,'mcol'=2] {'dp'}, dimensions={0}, use_global_device_ids=true | all-gather | bytes 540672 | tf_op jit(solution)/shard_map/all_gather | solution.py:38
  2128.6 0.5 bitcast_add_fusion
  2129.1 0.0 reduce-scatter.5.cloned.1.call-done
  2129.1 0.8 copy.12
  2129.9 0.0 copy-done.4
  (2 shorter events, 0.0 us)
Async XLA Ops:
  7.2 1.6 copy-start
  7.2 4.5 copy-start.1
  7.2 4.5 copy-start.2
  7.2 670.8 %reduce-scatter.3.cloned.1.call-start = ((), (), s32[]{:S(2)}) async-start(), calls=%async_computation.2 | async-start | bytes 1081344 | tf_op jit(solution)/shard_map/reduce_scatter | solution.py:11
  11.6 2.2 copy-start.3
  11.6 2.8 copy-start.5
  11.6 667.3 %copy-start.6 = (f32[1,1,1,32]{3,2,1,0:T(1,128)S(1)}, f32[1,1,1,32]{3,2,1,0:T(1,128)}, u32[]{:S(2)}) copy-start(f32[1,1,1,32]{3,2,1,0:T(1,128)} %param.10) | copy-start | bytes 388
  11.6 2117.6 %reduce-scatter.5.cloned.1.call-start = ((), (), s32[]{:S(2)}) async-start(), calls=%async_computation.3 | async-start | bytes 3145728 | tf_op jit(solution)/shard_map/reduce_scatter | solution.py:20
  1352.4 777.5 %copy-start.4 = (f32[256]{0:T(256)}, f32[256]{0:T(256)S(1)}, u32[]{:S(2)}) copy-start(f32[256]{0:T(256)S(1)} %multiply_add_fusion.1) | copy-start | bytes 3076
Sparse Core Ops, SparseCore 0:
  12.4 665.5 reduce-scatter.2
  681.6 17.0 reduce-scatter.4
where the time goes:
time: 2140 us
  blocking collectives  1440 us (67%)
  waiting for transfers between devices  664 us (31%)
    psum x1, blocking collectives, on_device(): update_sq = lax.psum(jnp.sum(update * update), ('dp', 'mrow'))  684 us
    psum x1, blocking collectives, on_device(): lax.psum((col_part, row_total, param_sq), ('dp', 'mrow'))  672 us
    reduce_scatter x1, waiting for transfers between devices, on_device(): lax.psum_scatter(lax.dot_general(inputs, kv_grads, (((0,), (0,)), ((), ()...  664 us
    all_gather x1, blocking collectives, on_device(): lax.all_gather(new_params.astype(jnp.bfloat16), 'dp', axis=0, tiled=True)  88.2 us
  transfers between devices with their start and end apart: 2, of which 1 were waited for; matrix products, arithmetic and copies ran while one was open for 0% of the time, Pallas kernels for 0%

commit v1 on v0

v1 whole, which is shorter than its diff:
```python
import jax
import jax.numpy as jnp
from jax import lax
from jax.experimental import pallas as pl
from jax.experimental.pallas import tpu as pltpu
from jax.sharding import PartitionSpec as P

D = 8192
HEAD = 256
MESH = pl.DeviceIdType.MESH
BF = jnp.bfloat16
F32 = jnp.float32

AGG = (-6, 6, -3, 3, 0)
FAR = AGG[:4]
NEAR = ((1, 1), (-1, 1), (1, 0), (-1, 0), (0, 1))
FAR_SIDE = ((2, 1), (2, 0))
XY = tuple((y, h, l) for y in range(4) for h in range(2) for l in range(2) if (y, h, l) != (0, 0, 0))
ZS = tuple(range(1, 16))
B = 32


def kernel(a_hbm, kv_hbm, w_hbm, m_ref, r_ref, c_ref,
           nm_ref, nr_ref, nc_ref, nw_ref, ig_hbm,
           a_v, kv, kvo, w_v, wo, ig_v, grad, s1_out, s1_in, s1_far, s2_out, s2_in,
           hbuf, pbuf, pnear, pfar, st1, st2,
           loc, core_s, core_r, a_s, a_r, b_s, b_r, c_s, c_r, d_s, d_r,
           p_s, p_r, q_s, q_r, x_s, x_r, z_s, z_r):
    dp = lax.axis_index("dp")
    mrow = lax.axis_index("mrow")
    core = lax.axis_index("mcol")
    z, xh = dp // 2, dp % 2
    y, xl = mrow // 2, mrow % 2

    def dev(dz=0, dx=0, dy=0, dl=0, dc=0):
        return (
            ((z + dz + 16) % 16) * 2 + (xh + dx) % 2,
            ((y + dy + 4) % 4) * 2 + (xl + dl) % 2,
            (core + dc) % 2,
        )

    def block(dz, dx):
        return ((z + dz + 32) % 16) * 2 + (xh + dx) % 2

    def rows(index):
        return pl.ds(pl.multiple_of(index * B, B), B)

    def send(src, dst, ssem, rsem, to):
        copy = pltpu.make_async_remote_copy(
            src_ref=src, dst_ref=dst, send_sem=ssem, recv_sem=rsem, device_id=to, device_id_type=MESH
        )
        copy.start()
        return copy

    def arrived(dst, ssem, rsem):
        pltpu.make_async_remote_copy(
            src_ref=dst, dst_ref=dst, send_sem=ssem, recv_sem=rsem, device_id=dev(dc=1), device_id_type=MESH
        ).wait_recv()

    load_kv = pltpu.make_async_copy(kv_hbm, kv, loc.at[0])
    load_a = pltpu.make_async_copy(a_hbm, a_v, loc.at[1])
    load_w = pltpu.make_async_copy(w_hbm, w_v, loc.at[2])
    load_kv.start()
    load_a.start()
    load_w.start()

    peers = [dev(dz=d) for d in ZS]
    peers += [dev(dy=py, dx=ph, dl=pl_) for py, ph, pl_ in XY]
    peers += [dev(dz=d, dx=1) for d in (1, -1, 2, -2)]
    peers += [dev(dc=1)]
    barrier = pltpu.get_barrier_semaphore()
    for to in peers:
        pl.semaphore_signal(barrier, inc=1, device_id=to, device_id_type=MESH)

    load_kv.wait()
    load_a.wait()

    def grad_step(i, _):
        cols = pl.ds(pl.multiple_of(i * 256, 256), 256)
        grad[cols, :] = lax.dot_general(
            a_v[:, cols], kv[...], (((0,), (0,)), ((), ())), preferred_element_type=F32
        )
        return 0

    lax.fori_loop(0, 4, grad_step, 0)
    for n, (o, x) in enumerate(NEAR):
        for j, a in enumerate(AGG):
            s1_out[n, j * B:(j + 1) * B, :] = grad[rows(block(o - a, x)), :].astype(BF)
    for n, (o, x) in enumerate(FAR_SIDE):
        s1_out[5 + n, 0:B, :] = grad[rows(block(-o - 6, x)), :].astype(BF)

    load_w.wait()
    pl.semaphore_wait(barrier, len(peers))

    sent = []
    for n, (o, x) in enumerate(NEAR):
        sent.append(send(s1_out.at[n], s1_in.at[n], a_s.at[n], a_r.at[n], dev(dz=o, dx=x)))
    for n, (o, x) in enumerate(FAR_SIDE):
        sent.append(send(s1_out.at[5 + n, pl.ds(0, B)], s1_far.at[n], a_s.at[5 + n], a_r.at[5 + n], dev(dz=-o, dx=x)))

    half = w_v.shape[0] // 2
    mine = pl.ds(pl.multiple_of(core * half, half), half)
    theirs = pl.ds(pl.multiple_of((1 - core) * half, half), half)
    sent.append(send(kv, kvo, core_s.at[0], core_r.at[0], dev(dc=1)))
    sent.append(send(w_v.at[theirs], wo, core_s.at[1], core_r.at[1], dev(dc=1)))

    params = m_ref[0, 0]
    pbuf[4] = params.astype(BF)
    for j, a in enumerate(FAR):
        sent.append(send(pbuf.at[4], pbuf.at[j], p_s.at[j], p_r.at[j], dev(dz=a)))

    arrived(kvo, core_s.at[0], core_r.at[0])
    arrived(wo, core_s.at[1], core_r.at[1])

    def ig_step(i, _):
        toks = pl.ds(pl.multiple_of(i * 256, 256), 256)
        dims = (((1,), (1,)), ((), ()))
        own = lax.dot_general(kv[toks, :], w_v[mine, :], dims, preferred_element_type=F32).astype(BF)
        other = lax.dot_general(kvo[toks, :], wo[...], dims, preferred_element_type=F32).astype(BF)
        ig_v[toks, :] = (own.astype(F32) + other.astype(F32)).astype(BF)
        return 0

    lax.fori_loop(0, 4, ig_step, 0)
    store_ig = pltpu.make_async_copy(ig_v, ig_hbm, loc.at[3])
    store_ig.start()

    for n in range(5):
        arrived(s1_in.at[n], a_s.at[n], a_r.at[n])
    for n in range(2):
        arrived(s1_far.at[n], a_s.at[5 + n], a_r.at[5 + n])
    total = None
    for j, a in enumerate(AGG):
        part = grad[rows(block(-a, 0)), :]
        for n in range(5):
            part = part + s1_in[n, j * B:(j + 1) * B, :].astype(F32)
        if a == 6:
            for n in range(2):
                part = part + s1_far[n].astype(F32)
        if a == 0:
            total = part
        else:
            s2_out[j] = part.astype(BF)
            sent.append(send(s2_out.at[j], s2_in.at[j], b_s.at[j], b_r.at[j], dev(dz=-a)))

    for j in range(4):
        arrived(pbuf.at[j], p_s.at[j], p_r.at[j])
    for n, (o, x) in enumerate(NEAR):
        sent.append(send(pbuf, pnear.at[n], q_s.at[n], q_r.at[n], dev(dz=o, dx=x)))
    for n, (o, x) in enumerate(FAR_SIDE):
        sent.append(send(pbuf.at[1], pfar.at[n], q_s.at[5 + n], q_r.at[5 + n], dev(dz=o, dx=x)))

    for j in range(4):
        arrived(s2_in.at[j], b_s.at[j], b_r.at[j])
        total = total + s2_in[j].astype(F32)
    g = total

    eye = (lax.broadcasted_iota(jnp.int32, (B, B), 0) == lax.broadcasted_iota(jnp.int32, (B, B), 1)).astype(F32)
    old_rows = jnp.sum(eye * r_ref[0, 0], axis=1, keepdims=True)
    sq = g * g + 1e-30
    new_rows = 0.8 * old_rows + 0.2 * (jnp.sum(sq, axis=1, keepdims=True) * (1.0 / HEAD))
    h = g / jnp.sqrt(new_rows)
    hbuf[rows(dp), :] = h.astype(BF)
    col = jnp.sum(sq, axis=0, keepdims=True)
    weighted = jnp.sum(h * h, axis=0, keepdims=True)
    my_xy = y * 4 + xh * 2 + xl
    one = jnp.ones((1, 128), F32)
    st1[my_xy] = jnp.concatenate(
        [col[:, :128], col[:, 128:], weighted[:, :128], weighted[:, 128:],
         one * jnp.sum(new_rows), one * jnp.sum(params * params), one, one], axis=0)
    for n, (py, ph, pl_) in enumerate(XY):
        sent.append(send(st1.at[my_xy], st1.at[my_xy], x_s.at[n], x_r.at[n], dev(dy=py, dx=ph, dl=pl_)))

    for j, a in enumerate(FAR):
        sent.append(send(hbuf.at[rows(dp)], hbuf.at[rows(dp)], c_s.at[j], c_r.at[j], dev(dz=a)))

    def forward(j):
        a = AGG[j]
        src = hbuf.at[rows(block(-a, 0))]
        for n, (o, x) in enumerate(NEAR):
            sent.append(send(src, src, d_s.at[j, n], d_r.at[j, n], dev(dz=o, dx=x)))
        if a == 6:
            for n, (o, x) in enumerate(FAR_SIDE):
                sent.append(send(src, src, d_s.at[5, n], d_r.at[5, n], dev(dz=o, dx=x)))

    forward(4)
    nr_ref[0, 0] = jnp.sum(eye * new_rows, axis=0, keepdims=True)
    for j in (2, 3):
        arrived(hbuf.at[rows(block(-AGG[j], 0))], c_s.at[j], c_r.at[j])
        forward(j)
    for n, (py, ph, pl_) in enumerate(XY):
        src = ((y - py + 4) % 4) * 4 + ((xh + ph) % 2) * 2 + (xl + pl_) % 2
        arrived(st1.at[src], x_s.at[n], x_r.at[n])
    plane = st1[0]
    for i in range(1, 16):
        plane = plane + st1[i]
    st2[z] = plane
    for n, d in enumerate(ZS):
        sent.append(send(st2.at[z], st2.at[z], z_s.at[n], z_r.at[n], dev(dz=d)))
    for j in (0, 1):
        arrived(hbuf.at[rows(block(-AGG[j], 0))], c_s.at[j], c_r.at[j])
        forward(j)
    for n, (o, x) in enumerate(NEAR):
        arrived(pnear.at[n], q_s.at[n], q_r.at[n])
    for n in range(2):
        arrived(pfar.at[n], q_s.at[5 + n], q_r.at[5 + n])
    for n, d in enumerate(ZS):
        arrived(st2.at[(z - d + 16) % 16], z_s.at[n], z_r.at[n])
    whole = st2[0]
    for i in range(1, 16):
        whole = whole + st2[i]
    col_sum = jnp.concatenate([whole[0:1], whole[1:2]], axis=1)
    weight_sum = jnp.concatenate([whole[2:3], whole[3:4]], axis=1)
    row_avg = whole[4:5, 0:1] / D
    param_rms = jnp.sqrt(whole[5:6, 0:1] / (D * HEAD))
    new_cols = 0.8 * c_ref[...] + 0.2 * col_sum / D
    nc_ref[...] = new_cols
    update_sq = row_avg * jnp.sum(weight_sum / new_cols, axis=1, keepdims=True)
    clip = jnp.maximum(1.0, jnp.sqrt(update_sq / (D * HEAD)))
    scale = (0.5 * param_rms / clip) * (jnp.sqrt(row_avg) / jnp.sqrt(new_cols))
    nm_ref[0, 0] = params - h * scale

    for j in range(5):
        for n, (o, x) in enumerate(NEAR):
            arrived(hbuf.at[rows(block(-o - AGG[j], x))], d_s.at[j, n], d_r.at[j, n])
    for n, (o, x) in enumerate(FAR_SIDE):
        arrived(hbuf.at[rows(block(-o - 6, x))], d_s.at[5, n], d_r.at[5, n])

    def finish(p, index):
        nw_ref[rows(index), :] = (p.astype(F32) - hbuf[rows(index), :].astype(F32) * scale).astype(BF)

    for j, a in enumerate(AGG):
        finish(pbuf[j], block(-a, 0))
        for n, (o, x) in enumerate(NEAR):
            finish(pnear[n, j], block(-o - a, x))
    for n, (o, x) in enumerate(FAR_SIDE):
        finish(pfar[n], block(-o - 6, x))

    for copy in sent:
        copy.wait_send()
    store_ig.wait()


def on_device(inputs, kv_grads, weight, master, row_state, col_state):
    vmem = pl.BlockSpec(memory_space=pltpu.VMEM)
    hbm = pl.BlockSpec(memory_space=pl.ANY)
    dma = pltpu.SemaphoreType.DMA
    return pl.pallas_call(
        kernel,
        out_shape=(
            jax.ShapeDtypeStruct((1, 1, 32, 256), F32),
            jax.ShapeDtypeStruct((1, 1, 1, 32), F32),
            jax.ShapeDtypeStruct((1, 256), F32),
            jax.ShapeDtypeStruct((1024, 256), BF),
            jax.ShapeDtypeStruct((1024, 512), BF),
        ),
        in_specs=[hbm, hbm, hbm, vmem, vmem, vmem],
        out_specs=(vmem, vmem, vmem, vmem, hbm),
        scratch_shapes=[
            pltpu.VMEM((1024, 1024), BF),
            pltpu.VMEM((1024, 256), BF),
            pltpu.VMEM((1024, 256), BF),
            pltpu.VMEM((1024, 256), BF),
            pltpu.VMEM((512, 256), BF),
            pltpu.VMEM((1024, 512), BF),
            pltpu.VMEM((1024, 256), F32),
            pltpu.VMEM((7, 5 * B, 256), BF),
            pltpu.VMEM((5, 5 * B, 256), BF),
            pltpu.VMEM((2, B, 256), BF),
            pltpu.VMEM((4, B, 256), BF),
            pltpu.VMEM((4, B, 256), BF),
            pltpu.VMEM((1024, 256), BF),
            pltpu.VMEM((5, B, 256), BF),
            pltpu.VMEM((5, 5, B, 256), BF),
            pltpu.VMEM((2, B, 256), BF),
            pltpu.VMEM((16, 8, 128), F32),
            pltpu.VMEM((16, 8, 128), F32),
            dma((4,)), dma((2,)), dma((2,)), dma((7,)), dma((7,)), dma((4,)), dma((4,)),
            dma((4,)), dma((4,)), dma((6, 5)), dma((6, 5)), dma((4,)), dma((4,)),
            dma((7,)), dma((7,)), dma((15,)), dma((15,)), dma((15,)), dma((15,)),
        ],
        compiler_params=pltpu.CompilerParams(
            collective_id=0, has_side_effects=True, vmem_limit_bytes=40 << 20
        ),
        name="kv_backward_adafactor",
    )(inputs, kv_grads, weight, master, row_state, col_state)


def solution(mesh):
    placed = (
        P("dp", "mrow"),
        P("dp", "mcol"),
        P("mrow", "mcol"),
        P("mrow", "dp", None, "mcol"),
        P("mcol", "mrow", "dp", None),
        P("mcol", None),
    )
    return jax.shard_map(
        on_device,
        mesh=mesh,
        in_specs=placed,
        out_specs=(
            P("mrow", "dp", None, "mcol"),
            P("mcol", "mrow", "dp", None),
            P("mcol", None),
            P("mrow", "mcol"),
            P("dp", ("mrow", "mcol")),
        ),
        check_vma=False,
    )
```

time: 2140 us -> 59.1 us (0.03)
  blocking collectives: 1440 us -> 0 us
  waiting for transfers between devices: 664 us -> 0 us
  Pallas kernels: 0 us -> 48.9 us
    psum x2 -> x0, blocking collectives: 1360 us -> none  [the longest x1 684 us: on_device(): update_sq = lax.psum(jnp.sum(update * update), ('dp', 'mrow'))]
    reduce_scatter x2 -> x0, waiting for transfers between devices: 664 us -> none  [the longest x1 664 us: on_device(): lax.psum_scatter(lax.dot_general(inputs, kv_grads, (((0,), (0,)), ((), ()...]
    all_gather x1 -> x0, blocking collectives: 88.2 us -> none  [on_device(): lax.all_gather(new_params.astype(jnp.bfloat16), 'dp', axis=0, tiled=True)]
    pallas_call x0 -> x1, Pallas kernels: none -> 48.9 us  [on_device(): pl.pallas_call(kernel, out_shape=(jax.ShapeDtypeStruct((1, 1, 32, 256), F...]
  transfers between devices with their start and end apart: 2 -> 0, of which waited for: 1 -> 0; matrix products, arithmetic and copies ran while one was open for 0% -> 0% of each run, Pallas kernels for 0% -> 0%
where the time goes in v1:
time: 59.1 us; the launch traced here: 58.7 us
  Pallas kernels  48.9 us (83%)
  local copies, waits for them, and re-layouts  9.21 us (16%)
  between operations  0.66 us (1%)
    pallas_call x1, Pallas kernels, on_device(): pl.pallas_call(kernel, out_shape=(jax.ShapeDtypeStruct((1, 1, 32, 256), F...  48.9 us
    unnamed x17, local copies, waits for them, and re-layouts  9.21 us

profile of v1, /device:TPU:24, one launch (start us, length us, event | category | flops | bytes accessed | tf_op | source)
XLA Modules:
  0.0 58.7 jit_solution(10023732681813523739)
XLA Ops:
  0.6 0.0 copy-start
  0.6 1.6 %copy-done = bf16[1024,1024]{1,0:T(8,128)(2,1)S(1)} copy-done((bf16[1024,1024]{1,0:T(8,128)(2,1)S(1)}, bf16[1024,1024]{1,0:T(8,128)(2,1)}, u32[]{:S(2)}) %copy-start) | copy-done | bytes 2097176
  2.2 0.0 copy-start.1
  2.2 1.0 %copy-done.1 = bf16[1024,256]{1,0:T(8,128)(2,1)S(1)} copy-done((bf16[1024,256]{1,0:T(8,128)(2,1)S(1)}, bf16[1024,256]{1,0:T(8,128)(2,1)}, u32[]{:S(2)}) %copy-start.1) | copy-done | bytes 524312
  3.3 0.0 copy-start.2
  3.3 1.0 %copy-done.2 = bf16[1024,256]{1,0:T(8,128)(2,1)S(1)} copy-done((bf16[1024,256]{1,0:T(8,128)(2,1)S(1)}, bf16[1024,256]{1,0:T(8,128)(2,1)}, u32[]{:S(2)}) %copy-start.2) | copy-done | bytes 524312
  4.3 0.0 copy-start.3
  4.3 0.8 %copy-done.3 = f32[1,1,32,256]{3,2,1,0:T(8,128)S(1)} copy-done((f32[1,1,32,256]{3,2,1,0:T(8,128)S(1)}, f32[1,1,32,256]{3,2,1,0:T(8,128)}, u32[]{:S(2)}) %copy-start.3) | copy-done | bytes 32792
  5.1 0.0 copy-start.4
  5.1 0.7 %copy-done.4 = f32[1,256]{1,0:T(1,128)S(1)} copy-done((f32[1,256]{1,0:T(1,128)S(1)}, f32[1,256]{1,0:T(1,128)}, u32[]{:S(2)}) %copy-start.4) | copy-done | bytes 1048
  5.7 0.0 copy-start.5
  5.7 0.7 %copy-done.5 = f32[1,1,1,32]{3,2,1,0:T(1,128)S(1)} copy-done((f32[1,1,1,32]{3,2,1,0:T(1,128)S(1)}, f32[1,1,1,32]{3,2,1,0:T(1,128)}, u32[]{:S(2)}) %copy-start.5) | copy-done | bytes 152
  6.4 48.9 %kv_backward_adafactor.1 = (f32[1,1,32,256]{3,2,1,0:T(8,128)S(1)}, f32[1,1,1,32]{3,2,1,0:T(1,128)S(1)}, f32[1,256]{1,0:T(1,128)S(1)}, bf16[1024,256]{1,0:T(8,128)(2,1)S(1)}, bf16[1024,512]{1,0:T(8,128)(2,1)S(1)}) custom-call(bf16[1024,1024]{1,0:T(8,128)(2,1)S(1)} %copy-done, bf16[1024,256]{1,0:T(8,128)(2,1)S(1)} %copy-done.1, ...), custom_call_target="tpu_custom_call" | custom-call | tf_op jit(solution)/shard_map/kv_backward_adafactor/pallas_call | solution.py:247
  55.3 0.6 %copy.16 = f32[1,1,32,256]{3,2,1,0:T(8,128)} copy(f32[1,1,32,256]{3,2,1,0:T(8,128)S(1)} %get-tuple-element.10) | data formatting | bytes 65536
  55.9 0.5 copy.17
  56.4 0.6 copy.18
  57.0 0.8 %copy.19 = bf16[1024,256]{1,0:T(8,128)(2,1)} copy(bf16[1024,256]{1,0:T(8,128)(2,1)S(1)} %get-tuple-element.13) | data formatting | bytes 1048576
  57.7 1.0 %copy.20 = bf16[1024,512]{1,0:T(8,128)(2,1)} copy(bf16[1024,512]{1,0:T(8,128)(2,1)S(1)} %get-tuple-element.14) | data formatting | bytes 2097152
Async XLA Ops:
  0.6 1.6 %copy-start = (bf16[1024,1024]{1,0:T(8,128)(2,1)S(1)}, bf16[1024,1024]{1,0:T(8,128)(2,1)}, u32[]{:S(2)}) copy-start(bf16[1024,1024]{1,0:T(8,128)(2,1)} %a_hbm.1) | copy-start | bytes 6291460
  2.2 1.0 %copy-start.1 = (bf16[1024,256]{1,0:T(8,128)(2,1)S(1)}, bf16[1024,256]{1,0:T(8,128)(2,1)}, u32[]{:S(2)}) copy-start(bf16[1024,256]{1,0:T(8,128)(2,1)} %kv_hbm.1) | copy-start | bytes 1572868
  3.3 1.0 %copy-start.2 = (bf16[1024,256]{1,0:T(8,128)(2,1)S(1)}, bf16[1024,256]{1,0:T(8,128)(2,1)}, u32[]{:S(2)}) copy-start(bf16[1024,256]{1,0:T(8,128)(2,1)} %w_hbm.1) | copy-start | bytes 1572868
  4.3 0.8 %copy-start.3 = (f32[1,1,32,256]{3,2,1,0:T(8,128)S(1)}, f32[1,1,32,256]{3,2,1,0:T(8,128)}, u32[]{:S(2)}) copy-start(f32[1,1,32,256]{3,2,1,0:T(8,128)} %m_ref.1) | copy-start | bytes 98308
  5.1 0.7 %copy-start.4 = (f32[1,256]{1,0:T(1,128)S(1)}, f32[1,256]{1,0:T(1,128)}, u32[]{:S(2)}) copy-start(f32[1,256]{1,0:T(1,128)} %c_ref.1) | copy-start | bytes 3076
  5.7 0.7 %copy-start.5 = (f32[1,1,1,32]{3,2,1,0:T(1,128)S(1)}, f32[1,1,1,32]{3,2,1,0:T(1,128)}, u32[]{:S(2)}) copy-start(f32[1,1,1,32]{3,2,1,0:T(1,128)} %r_ref.1) | copy-start | bytes 388

commit v2 on v0

v2 whole, which is shorter than its diff:
```python
import jax
import jax.numpy as jnp
from jax import lax
from jax.experimental import pallas as pl
from jax.experimental.pallas import tpu as pltpu
from jax.sharding import PartitionSpec as P

D = 8192
HEAD = 256
MESH = pl.DeviceIdType.MESH
BF = jnp.bfloat16
F32 = jnp.float32

AGG = (-6, 6, -3, 3, 0)
FAR = AGG[:4]
NEAR = ((1, 1), (-1, 1), (1, 0), (-1, 0), (0, 1))
SIDE = ((2, 1), (2, 0))
XY = ((2, 1, 1), (1, 1, 1), (3, 1, 1), (2, 1, 0), (2, 0, 1), (1, 1, 0), (3, 1, 0), (0, 1, 1),
      (2, 0, 0), (1, 0, 1), (3, 0, 1), (0, 1, 0), (1, 0, 0), (3, 0, 0), (0, 0, 1))
ZS = (8, 7, 9, 6, 10, 5, 11, 4, 12, 3, 13, 2, 14, 1, 15)
B = 32


def kernel(a_hbm, kv_hbm, w_hbm, m_hbm, r_hbm, c_hbm,
           nm_ref, nr_ref, nc_ref, nw_ref, ig_ref,
           m_ref, r_ref, c_ref, a_v, kv, kvo, w_v, wo, grad,
           f_out, f_in, n_out, n_in, side_out, side_in, s2_out, s2_in,
           hbuf, pbuf, pz, pfar, st1, st2, loc, core_s, core_r,
           f_s, f_r, n_s, n_r, side_s, side_r, b_s, b_r, c_s, c_r, d_s, d_r, e_s, e_r,
           p_s, p_r, px_s, px_r, q_s, q_r, qf_s, qf_r, x_s, x_r, z_s, z_r, known3, known6, plane1, plane2):
    dp = lax.axis_index("dp")
    mrow = lax.axis_index("mrow")
    core = lax.axis_index("mcol")
    z, xh = lax.div(dp, 2), lax.rem(dp, 2)
    y, xl = lax.div(mrow, 2), lax.rem(mrow, 2)
    at_x = (xh, 1 - xh)
    at_l = (xl, 1 - xl)
    at_z = [z] + [lax.rem(z + d, 16) for d in range(1, 16)]
    at_y = [y] + [lax.rem(y + d, 4) for d in range(1, 4)]
    at_dp = [[at_z[d] * 2 + at_x[x] for x in range(2)] for d in range(16)]
    at_mrow = [[at_y[d] * 2 + at_l[l] for l in range(2)] for d in range(4)]
    at_core = (core, 1 - core)
    at_rows = [[pl.multiple_of(at_dp[d][x] * B, B) for x in range(2)] for d in range(16)]

    def dev(dz=0, dx=0, dy=0, dl=0, dc=0):
        return at_dp[dz % 16][dx], at_mrow[dy % 4][dl], at_core[dc]

    def rows(dz, dx):
        return pl.ds(at_rows[dz % 16][dx], B)

    sent, pending = [], {}

    def send(src, dst, sems, n, to):
        copy = pltpu.make_async_remote_copy(
            src_ref=src, dst_ref=dst, send_sem=sems[0].at[n], recv_sem=sems[1].at[n],
            device_id=to, device_id_type=MESH,
        )
        copy.start()
        sent.append(copy)
        pending[id(sems[1]), n] = copy

    def arrived(dst, sems, n):
        pltpu.make_async_remote_copy(
            src_ref=dst, dst_ref=dst, send_sem=sems[0].at[n], recv_sem=sems[1].at[n],
            device_id=dev(dc=1), device_id_type=MESH,
        ).wait_recv()
        del pending[id(sems[1]), n]

    loads = [
        pltpu.make_async_copy(src, dst, loc.at[i])
        for i, (src, dst) in enumerate(
            ((kv_hbm, kv), (w_hbm, w_v), (m_hbm, m_ref), (r_hbm, r_ref), (c_hbm, c_ref)))
    ]
    chunks = [pl.ds(i * 256, 256) for i in range(4)]
    loads_a = [pltpu.make_async_copy(a_hbm.at[:, c], a_v.at[:, c], loc.at[5 + i]) for i, c in enumerate(chunks)]
    loads[0].start()
    for copy in loads_a + loads[1:]:
        copy.start()

    peers = [dev(dz=d, dx=x) for d in (1, -1, 2, -2) for x in (0, 1)]
    peers += [dev(dz=d) for d in (3, -3)]
    peers += [dev(dx=1), dev(dy=1), dev(dy=-1), dev(dl=1), dev(dc=1)]
    barrier = pltpu.get_barrier_semaphore()
    for to in peers:
        pl.semaphore_signal(barrier, inc=1, device_id=to, device_id_type=MESH)

    loads[0].wait()
    for copy, c in zip(loads_a, chunks):
        copy.wait()
        grad[c, :] = lax.dot_general(
            a_v[:, c], kv[...], (((0,), (0,)), ((), ())), preferred_element_type=F32
        )
    for n, (o, x) in enumerate(SIDE):
        side_out[n] = grad[rows(-o - 6, x), :].astype(BF)
    for n, (o, x) in enumerate(NEAR):
        for j in range(2):
            f_out[n, j * B:(j + 1) * B, :] = grad[rows(o - AGG[j], x), :].astype(BF)
        for j in range(3):
            n_out[n, j * B:(j + 1) * B, :] = grad[rows(o - AGG[2 + j], x), :].astype(BF)

    for copy in loads[1:]:
        copy.wait()
    pl.semaphore_wait(barrier, len(peers))

    for n, (o, x) in enumerate(SIDE):
        send(side_out.at[n], side_in.at[n], (side_s, side_r), n, dev(dz=-o, dx=x))
    for n, (o, x) in enumerate(NEAR):
        send(f_out.at[n], f_in.at[n], (f_s, f_r), n, dev(dz=o, dx=x))
    for d in (3, -3):
        pl.semaphore_signal(known3, inc=1, device_id=dev(dz=d), device_id_type=MESH)
    for to in (dev(dy=1), dev(dy=-1), dev(dl=1), dev(dx=1)):
        pl.semaphore_signal(plane1, inc=1, device_id=to, device_id_type=MESH)
    for n, (o, x) in enumerate(NEAR):
        send(n_out.at[n], n_in.at[n], (n_s, n_r), n, dev(dz=o, dx=x))

    params = m_ref[0, 0]
    pbuf[4] = params.astype(BF)
    for j in (2, 3):
        send(pbuf.at[4], pbuf.at[j], (p_s, p_r), j, dev(dz=AGG[j]))
    pl.semaphore_wait(known3, 2)
    for d in (6, -6):
        pl.semaphore_signal(known6, inc=1, device_id=dev(dz=d), device_id_type=MESH)
    for j in (0, 1):
        send(pbuf.at[4], pbuf.at[j], (p_s, p_r), j, dev(dz=AGG[j]))
    pl.semaphore_wait(plane1, 4)
    for d in (1, -1, 2):
        pl.semaphore_signal(plane2, inc=1, device_id=dev(dy=d), device_id_type=MESH)
    half = w_v.shape[0] // 2
    mine = pl.ds(pl.multiple_of(core * half, half), half)
    theirs = pl.ds(pl.multiple_of((1 - core) * half, half), half)
    send(kv, kvo, (core_s, core_r), 0, dev(dc=1))
    send(w_v.at[theirs], wo, (core_s, core_r), 1, dev(dc=1))

    def aggregate(j):
        a = AGG[j]
        part = grad[rows(-a, 0), :]
        for n in range(5):
            got = f_in[n, j * B:(j + 1) * B, :] if j < 2 else n_in[n, (j - 2) * B:(j - 1) * B, :]
            part = part + got.astype(F32)
        if a == 6:
            for n in range(2):
                part = part + side_in[n].astype(F32)
        if a == 0:
            return part
        s2_out[j] = part.astype(BF)
        send(s2_out.at[j], s2_in.at[j], (b_s, b_r), j, dev(dz=-a))

    for n in range(2):
        arrived(side_in.at[n], (side_s, side_r), n)
    for n in range(5):
        arrived(f_in.at[n], (f_s, f_r), n)
    aggregate(0)
    aggregate(1)
    for n in range(5):
        arrived(n_in.at[n], (n_s, n_r), n)
    aggregate(2)
    aggregate(3)
    total = aggregate(4)

    for j in range(4):
        arrived(pbuf.at[j], (p_s, p_r), j)
    send(pbuf.at[pl.ds(0, 5)], pbuf.at[pl.ds(5, 5)], (px_s, px_r), 0, dev(dx=1))

    arrived(kvo, (core_s, core_r), 0)
    arrived(wo, (core_s, core_r), 1)

    def ig_step(i, _):
        toks = pl.ds(pl.multiple_of(i * 256, 256), 256)
        dims = (((1,), (1,)), ((), ()))
        own = lax.dot_general(kv[toks, :], w_v[mine, :], dims, preferred_element_type=F32).astype(BF)
        other = lax.dot_general(kvo[toks, :], wo[...], dims, preferred_element_type=F32).astype(BF)
        ig_ref[toks, :] = (own.astype(F32) + other.astype(F32)).astype(BF)
        return 0

    lax.fori_loop(0, 4, ig_step, 0)
    for copy in sent:
        copy.wait_send()
    sent.clear()
    for j in (2, 3, 0, 1):
        arrived(s2_in.at[j], (b_s, b_r), j)
        total = total + s2_in[j].astype(F32)
    g = total

    eye = (lax.broadcasted_iota(jnp.int32, (B, B), 0) == lax.broadcasted_iota(jnp.int32, (B, B), 1)).astype(F32)
    old_rows = jnp.sum(eye * r_ref[0, 0], axis=1, keepdims=True)
    sq = g * g + 1e-30
    new_rows = 0.8 * old_rows + 0.2 * (jnp.sum(sq, axis=1, keepdims=True) * (1.0 / HEAD))
    h = g / jnp.sqrt(new_rows)
    hbuf[rows(0, 0), :] = h.astype(BF)
    col = jnp.sum(sq, axis=0, keepdims=True)
    weighted = jnp.sum(h * h, axis=0, keepdims=True)
    pl.semaphore_wait(plane2, 3)
    my_xy = y * 4 + xh * 2 + xl
    left = lax.broadcasted_iota(jnp.int32, (1, 128), 1) < 64
    st1[my_xy] = jnp.concatenate(
        [col[:, :128], col[:, 128:], weighted[:, :128], weighted[:, 128:],
         jnp.where(left, jnp.sum(new_rows), jnp.sum(params * params))], axis=0)
    for n, (py, ph, pl_) in enumerate(XY):
        send(st1.at[my_xy], st1.at[my_xy], (x_s, x_r), n, dev(dy=py, dx=ph, dl=pl_))

    for j, a in enumerate(FAR):
        send(hbuf.at[rows(0, 0)], hbuf.at[rows(0, 0)], (c_s, c_r), j, dev(dz=a))

    def forward(j):
        src = hbuf.at[rows(-AGG[j], 0)]
        for n, (o, x) in enumerate(NEAR):
            send(src, src, (d_s, d_r), j * 5 + n, dev(dz=o, dx=x))
        if AGG[j] == 6:
            for n, (o, x) in enumerate(SIDE):
                send(src, src, (e_s, e_r), n, dev(dz=o, dx=x))

    forward(4)
    arrived(pbuf.at[pl.ds(5, 5)], (px_s, px_r), 0)
    for n in range(2):
        send(pbuf.at[5 * n + 1], pfar.at[n], (qf_s, qf_r), n, dev(dz=2))
    for n, o in enumerate((1, -1)):
        send(pbuf, pz.at[n], (q_s, q_r), n, dev(dz=o))
    nr_ref[0, 0] = jnp.sum(eye * new_rows, axis=0, keepdims=True)
    pl.semaphore_wait(known6, 2)
    for j in (2, 3):
        arrived(hbuf.at[rows(-AGG[j], 0)], (c_s, c_r), j)
        forward(j)
    for n, (py, ph, pl_) in enumerate(XY):
        src = at_y[-py % 4] * 4 + at_x[ph] * 2 + at_l[pl_]
        arrived(st1.at[src], (x_s, x_r), n)
    plane = st1[0]
    for i in range(1, 16):
        plane = plane + st1[i]
    st2[z] = plane
    early = len(sent)
    for n, d in enumerate(ZS):
        send(st2.at[z], st2.at[z], (z_s, z_r), n, dev(dz=d))
    for j in (0, 1):
        arrived(hbuf.at[rows(-AGG[j], 0)], (c_s, c_r), j)
        forward(j)

    for copy in sent[:early]:
        copy.wait_send()
    del sent[:early]
    for j in (4, 2, 3):
        for n, (o, x) in enumerate(NEAR):
            arrived(hbuf.at[rows(-o - AGG[j], x)], (d_s, d_r), j * 5 + n)
    for n, d in enumerate(ZS):
        arrived(st2.at[at_z[-d % 16]], (z_s, z_r), n)
    whole = st2[0]
    for i in range(1, 16):
        whole = whole + st2[i]
    col_sum = jnp.concatenate([whole[0:1], whole[1:2]], axis=1)
    weight_sum = jnp.concatenate([whole[2:3], whole[3:4]], axis=1)
    row_avg = whole[4:5, 0:1] / D
    param_rms = jnp.sqrt(whole[4:5, 64:65] / (D * HEAD))
    new_cols = 0.8 * c_ref[...] + 0.2 * col_sum / D
    nc_ref[...] = new_cols
    update_sq = row_avg * jnp.sum(weight_sum / new_cols, axis=1, keepdims=True)
    clip = jnp.maximum(1.0, jnp.sqrt(update_sq / (D * HEAD)))
    scale = (0.5 * param_rms / clip) * (jnp.sqrt(row_avg) / jnp.sqrt(new_cols))
    nm_ref[0, 0] = params - h * scale

    for j in range(2):
        for n, (o, x) in enumerate(NEAR):
            arrived(hbuf.at[rows(-o - AGG[j], x)], (d_s, d_r), j * 5 + n)
    for n, (o, x) in enumerate(SIDE):
        arrived(hbuf.at[rows(-o - 6, x)], (e_s, e_r), n)
    for n, o in enumerate((1, -1)):
        arrived(pz.at[n], (q_s, q_r), n)
    for n in range(2):
        arrived(pfar.at[n], (qf_s, qf_r), n)

    def finish(p, index):
        nw_ref[index, :] = (p.astype(F32) - hbuf[index, :].astype(F32) * scale).astype(BF)

    for x in range(2):
        for j, a in enumerate(AGG):
            finish(pbuf[5 * x + j], rows(-a, x))
            for n, o in enumerate((1, -1)):
                finish(pz[n, 5 * x + j], rows(-o - a, x))
        finish(pfar[x], rows(-8, x))

    for copy in sent:
        copy.wait_send()


def hand_over(*refs):
    n = len(refs) // 2
    sems = refs[-1]
    copies = [pltpu.make_async_copy(refs[i], refs[n + i], sems.at[i]) for i in range(n)]
    for copy in copies:
        copy.start()
    for copy in copies:
        copy.wait()


def on_device(inputs, kv_grads, weight, master, row_state, col_state):
    hbm = pl.BlockSpec(memory_space=pltpu.HBM)
    anywhere = pl.BlockSpec(memory_space=pl.ANY)
    vmem = pl.BlockSpec(memory_space=pltpu.VMEM)
    dma = pltpu.SemaphoreType.DMA
    out_shape = (
        jax.ShapeDtypeStruct((1, 1, 32, 256), F32),
        jax.ShapeDtypeStruct((1, 1, 1, 32), F32),
        jax.ShapeDtypeStruct((1, 256), F32),
        jax.ShapeDtypeStruct((1024, 256), BF),
        jax.ShapeDtypeStruct((1024, 512), BF),
    )
    results = pl.pallas_call(
        kernel,
        out_shape=out_shape,
        in_specs=[hbm] * 6,
        out_specs=(vmem,) * 5,
        scratch_shapes=[
            pltpu.VMEM((1, 1, 32, 256), F32),
            pltpu.VMEM((1, 1, 1, 32), F32),
            pltpu.VMEM((1, 256), F32),
            pltpu.VMEM((1024, 1024), BF),
            pltpu.VMEM((1024, 256), BF),
            pltpu.VMEM((1024, 256), BF),
            pltpu.VMEM((1024, 256), BF),
            pltpu.VMEM((512, 256), BF),
            pltpu.VMEM((1024, 256), F32),
            pltpu.VMEM((5, 2 * B, 256), BF),
            pltpu.VMEM((5, 2 * B, 256), BF),
            pltpu.VMEM((5, 3 * B, 256), BF),
            pltpu.VMEM((5, 3 * B, 256), BF),
            pltpu.VMEM((2, B, 256), BF),
            pltpu.VMEM((2, B, 256), BF),
            pltpu.VMEM((4, B, 256), BF),
            pltpu.VMEM((4, B, 256), BF),
            pltpu.VMEM((1024, 256), BF),
            pltpu.VMEM((10, B, 256), BF),
            pltpu.VMEM((2, 10, B, 256), BF),
            pltpu.VMEM((2, B, 256), BF),
            pltpu.VMEM((16, 5, 128), F32),
            pltpu.VMEM((16, 5, 128), F32),
            dma((9,)),
        ] + [dma((n,)) for n in (2, 5, 5, 2, 4, 4, 25, 2, 4, 1, 2, 2, 15, 15) for _ in range(2)] + [
            pltpu.SemaphoreType.REGULAR] + [pltpu.SemaphoreType.REGULAR] * 3,
        compiler_params=pltpu.CompilerParams(
            collective_id=0, has_side_effects=True, vmem_limit_bytes=24 << 20
        ),
        name="kv_backward_adafactor",
    )(*[pltpu.with_memory_space_constraint(x, pltpu.HBM) for x in (inputs, kv_grads, weight, master, row_state, col_state)])
    return pl.pallas_call(
        hand_over,
        out_shape=out_shape,
        in_specs=[anywhere] * 5,
        out_specs=(hbm,) * 5,
        scratch_shapes=[dma((5,))],
        compiler_params=pltpu.CompilerParams(vmem_limit_bytes=16 << 20),
        name="hand_over",
    )(*results)


def solution(mesh):
    placed = (
        P("dp", "mrow"),
        P("dp", "mcol"),
        P("mrow", "mcol"),
        P("mrow", "dp", None, "mcol"),
        P("mcol", "mrow", "dp", None),
        P("mcol", None),
    )
    return jax.shard_map(
        on_device,
        mesh=mesh,
        in_specs=placed,
        out_specs=(
            P("mrow", "dp", None, "mcol"),
            P("mcol", "mrow", "dp", None),
            P("mcol", None),
            P("mrow", "mcol"),
            P("dp", ("mrow", "mcol")),
        ),
        check_vma=False,
    )
```

time: 2140 us -> 49.2 us (0.02)
  blocking collectives: 1440 us -> 0 us
  waiting for transfers between devices: 664 us -> 0 us
  Pallas kernels: 0 us -> 48.4 us
    psum x2 -> x0, blocking collectives: 1360 us -> none  [the longest x1 684 us: on_device(): update_sq = lax.psum(jnp.sum(update * update), ('dp', 'mrow'))]
    reduce_scatter x2 -> x0, waiting for transfers between devices: 664 us -> none  [the longest x1 664 us: on_device(): lax.psum_scatter(lax.dot_general(inputs, kv_grads, (((0,), (0,)), ((), ()...]
    all_gather x1 -> x0, blocking collectives: 88.2 us -> none  [on_device(): lax.all_gather(new_params.astype(jnp.bfloat16), 'dp', axis=0, tiled=True)]
    pallas_call x0 -> x2, Pallas kernels: none -> 48.4 us  [the longest x1 47.2 us: on_device(): pl.pallas_call(kernel, out_shape=out_shape, in_specs=[hbm] * 6, out_specs...]
  transfers between devices with their start and end apart: 2 -> 0, of which waited for: 1 -> 0; matrix products, arithmetic and copies ran while one was open for 0% -> 0% of each run, Pallas kernels for 0% -> 0%
where the time goes in v2:
time: 49.2 us; the launch traced here: 49.1 us
  Pallas kernels  48.4 us (98%)
  between operations  0.64 us (1%)
    pallas_call x1, Pallas kernels, on_device(): pl.pallas_call(kernel, out_shape=out_shape, in_specs=[hbm] * 6, out_specs...  47.2 us
    pallas_call x1, Pallas kernels, on_device(): pl.pallas_call(hand_over, out_shape=out_shape, in_specs=[anywhere] * 5, o...  1.21 us

profile of v2, /device:TPU:24, one launch (start us, length us, event | category | flops | bytes accessed | tf_op | source)
XLA Modules:
  0.0 49.1 jit_solution(11002178601983196913)
XLA Ops:
  0.6 47.2 %kv_backward_adafactor.1 = (f32[1,1,32,256]{3,2,1,0:T(8,128)S(1)}, f32[1,1,1,32]{3,2,1,0:T(1,128)S(1)}, f32[1,256]{1,0:T(1,128)S(1)}, bf16[1024,256]{1,0:T(8,128)(2,1)S(1)}, bf16[1024,512]{1,0:T(8,128)(2,1)S(1)}) custom-call(bf16[1024,1024]{1,0:T(8,128)(2,1)} %a_hbm.1, bf16[1024,256]{1,0:T(8,128)(2,1)} %kv_hbm.1, bf16[1024,256]{1,0:T(8,128)(2,1)} %w_hbm.1, ...), custom_call_target="tpu_custom_call" | custom-call | tf_op jit(solution)/shard_map/kv_backward_adafactor/pallas_call | solution.py:305
  47.9 1.2 %hand_over.1 = (f32[1,1,32,256]{3,2,1,0:T(8,128)}, f32[1,1,1,32]{3,2,1,0:T(1,128)}, f32[1,256]{1,0:T(1,128)}, bf16[1024,256]{1,0:T(8,128)(2,1)}, bf16[1024,512]{1,0:T(8,128)(2,1)}) custom-call(f32[1,1,32,256]{3,2,1,0:T(8,128)S(1)} %get-tuple-element.10.refs_0_, f32[1,1,1,32]{3,2,1,0:T(1,128)S(1)} %get-tuple-element.11.refs_1_, ...), custom_call_target="tpu_custom_call" | custom-call | tf_op jit(solution)/shard_map/hand_over/pallas_call | solution.py:342

commit v3 on v2

--- a/solution.py
+++ b/solution.py
@@ -27,7 +27,7 @@
            f_out, f_in, n_out, n_in, side_out, side_in, s2_out, s2_in,
            hbuf, pbuf, pz, pfar, st1, st2, loc, core_s, core_r,
            f_s, f_r, n_s, n_r, side_s, side_r, b_s, b_r, c_s, c_r, d_s, d_r, e_s, e_r,
-           p_s, p_r, px_s, px_r, q_s, q_r, qf_s, qf_r, x_s, x_r, z_s, z_r, known3, known6, plane1, plane2):
+           po_s, po_r, p_s, p_r, px_s, px_r, q_s, q_r, qf_s, qf_r, pb_s, pb_r, x_s, x_r, z_s, z_r, known3, known6, plane1, plane2):
     dp = lax.axis_index("dp")
     mrow = lax.axis_index("mrow")
     core = lax.axis_index("mcol")
@@ -48,23 +48,28 @@
     def rows(dz, dx):
         return pl.ds(at_rows[dz % 16][dx], B)
 
-    sent, pending = [], {}
-
-    def send(src, dst, sems, n, to):
+    sent = []
+
+    def send(src, dst, sems, n, to, later=None):
         copy = pltpu.make_async_remote_copy(
             src_ref=src, dst_ref=dst, send_sem=sems[0].at[n], recv_sem=sems[1].at[n],
             device_id=to, device_id_type=MESH,
         )
         copy.start()
-        sent.append(copy)
-        pending[id(sems[1]), n] = copy
+        if later is None:
+            sent.append(copy)
+
+    def left(src, sems, n):
+        pltpu.make_async_remote_copy(
+            src_ref=src, dst_ref=src, send_sem=sems[0].at[n], recv_sem=sems[1].at[n],
+            device_id=dev(dc=1), device_id_type=MESH,
+        ).wait_send()
 
     def arrived(dst, sems, n):
         pltpu.make_async_remote_copy(
             src_ref=dst, dst_ref=dst, send_sem=sems[0].at[n], recv_sem=sems[1].at[n],
             device_id=dev(dc=1), device_id_type=MESH,
         ).wait_recv()
-        del pending[id(sems[1]), n]
 
     loads = [
         pltpu.make_async_copy(src, dst, loc.at[i])
@@ -114,14 +119,23 @@
         send(n_out.at[n], n_in.at[n], (n_s, n_r), n, dev(dz=o, dx=x))
 
     params = m_ref[0, 0]
-    pbuf[4] = params.astype(BF)
-    for j in (2, 3):
-        send(pbuf.at[4], pbuf.at[j], (p_s, p_r), j, dev(dz=AGG[j]))
+    pbuf[4, core] = params.astype(BF)
+
+    @pl.when(core == 0)
+    def _():
+        send(pbuf.at[4, 0], pbuf.at[4, 0], (po_s, po_r), 0, dev(dc=1), ())
+        left(pbuf.at[4, 0], (po_s, po_r), 0)
+
     pl.semaphore_wait(known3, 2)
     for d in (6, -6):
         pl.semaphore_signal(known6, inc=1, device_id=dev(dz=d), device_id_type=MESH)
-    for j in (0, 1):
-        send(pbuf.at[4], pbuf.at[j], (p_s, p_r), j, dev(dz=AGG[j]))
+
+    @pl.when(core == 1)
+    def _():
+        arrived(pbuf.at[4, 0], (po_s, po_r), 0)
+        for j, a in enumerate(FAR):
+            send(pbuf.at[4], pbuf.at[j], (p_s, p_r), j, dev(dz=a), ())
+
     pl.semaphore_wait(plane1, 4)
     for d in (1, -1, 2):
         pl.semaphore_signal(plane2, inc=1, device_id=dev(dy=d), device_id_type=MESH)
@@ -157,9 +171,23 @@
     aggregate(3)
     total = aggregate(4)
 
-    for j in range(4):
-        arrived(pbuf.at[j], (p_s, p_r), j)
-    send(pbuf.at[pl.ds(0, 5)], pbuf.at[pl.ds(5, 5)], (px_s, px_r), 0, dev(dx=1))
+    @pl.when(core == 1)
+    def _():
+        for j in range(4):
+            arrived(pbuf.at[j], (p_s, p_r), j)
+        send(pbuf.at[pl.ds(0, 5)], pbuf.at[pl.ds(5, 5)], (px_s, px_r), 0, dev(dx=1), ())
+
+    def third(x):
+        if x == 1:
+            arrived(pbuf.at[pl.ds(5, 5)], (px_s, px_r), 0)
+        send(pbuf.at[5 * x + 1], pfar.at[x], (qf_s, qf_r), x, dev(dz=2), ())
+        for n, o in enumerate((1, -1)):
+            part = pl.ds(5 * x, 5)
+            send(pbuf.at[part], pz.at[n, part], (q_s, q_r), 2 * n + x, dev(dz=o), ())
+
+    @pl.when(core == 1)
+    def _():
+        third(0)
 
     arrived(kvo, (core_s, core_r), 0)
     arrived(wo, (core_s, core_r), 1)
@@ -191,10 +219,10 @@
     weighted = jnp.sum(h * h, axis=0, keepdims=True)
     pl.semaphore_wait(plane2, 3)
     my_xy = y * 4 + xh * 2 + xl
-    left = lax.broadcasted_iota(jnp.int32, (1, 128), 1) < 64
+    low = lax.broadcasted_iota(jnp.int32, (1, 128), 1) < 64
     st1[my_xy] = jnp.concatenate(
         [col[:, :128], col[:, 128:], weighted[:, :128], weighted[:, 128:],
-         jnp.where(left, jnp.sum(new_rows), jnp.sum(params * params))], axis=0)
+         jnp.where(low, jnp.sum(new_rows), jnp.sum(params * params))], axis=0)
     for n, (py, ph, pl_) in enumerate(XY):
         send(st1.at[my_xy], st1.at[my_xy], (x_s, x_r), n, dev(dy=py, dx=ph, dl=pl_))
 
@@ -210,11 +238,10 @@
                 send(src, src, (e_s, e_r), n, dev(dz=o, dx=x))
 
     forward(4)
-    arrived(pbuf.at[pl.ds(5, 5)], (px_s, px_r), 0)
-    for n in range(2):
-        send(pbuf.at[5 * n + 1], pfar.at[n], (qf_s, qf_r), n, dev(dz=2))
-    for n, o in enumerate((1, -1)):
-        send(pbuf, pz.at[n], (q_s, q_r), n, dev(dz=o))
+    @pl.when(core == 1)
+    def _():
+        third(1)
+
     nr_ref[0, 0] = jnp.sum(eye * new_rows, axis=0, keepdims=True)
     pl.semaphore_wait(known6, 2)
     for j in (2, 3):
@@ -237,6 +264,15 @@
     for copy in sent[:early]:
         copy.wait_send()
     del sent[:early]
+    @pl.when(core == 1)
+    def _():
+        for x in range(2):
+            arrived(pfar.at[x], (qf_s, qf_r), x)
+            for n in range(2):
+                arrived(pz.at[n, pl.ds(5 * x, 5)], (q_s, q_r), 2 * n + x)
+        for i, part in enumerate((pbuf.at[:, 0], pz.at[:, :, 0], pfar.at[:, 0])):
+            send(part, part, (pb_s, pb_r), i, dev(dc=1), ())
+
     for j in (4, 2, 3):
         for n, (o, x) in enumerate(NEAR):
             arrived(hbuf.at[rows(-o - AGG[j], x)], (d_s, d_r), j * 5 + n)
@@ -261,20 +297,32 @@
             arrived(hbuf.at[rows(-o - AGG[j], x)], (d_s, d_r), j * 5 + n)
     for n, (o, x) in enumerate(SIDE):
         arrived(hbuf.at[rows(-o - 6, x)], (e_s, e_r), n)
-    for n, o in enumerate((1, -1)):
-        arrived(pz.at[n], (q_s, q_r), n)
-    for n in range(2):
-        arrived(pfar.at[n], (qf_s, qf_r), n)
+    for i in range(3):
+        @pl.when(core == 0)
+        def _():
+            arrived((pbuf.at[:, 0], pz.at[:, :, 0], pfar.at[:, 0])[i], (pb_s, pb_r), i)
 
     def finish(p, index):
         nw_ref[index, :] = (p.astype(F32) - hbuf[index, :].astype(F32) * scale).astype(BF)
 
     for x in range(2):
         for j, a in enumerate(AGG):
-            finish(pbuf[5 * x + j], rows(-a, x))
+            finish(pbuf[5 * x + j, core], rows(-a, x))
             for n, o in enumerate((1, -1)):
-                finish(pz[n, 5 * x + j], rows(-o - a, x))
-        finish(pfar[x], rows(-8, x))
+                finish(pz[n, 5 * x + j, core], rows(-o - a, x))
+        finish(pfar[x, core], rows(-8, x))
+
+    @pl.when(core == 1)
+    def _():
+        for j in range(4):
+            left(pbuf.at[j], (p_s, p_r), j)
+        left(pbuf.at[pl.ds(0, 5)], (px_s, px_r), 0)
+        for x in range(2):
+            left(pfar.at[x], (qf_s, qf_r), x)
+            for n in range(2):
+                left(pz.at[n, pl.ds(5 * x, 5)], (q_s, q_r), 2 * n + x)
+        for i, part in enumerate((pbuf.at[:, 0], pz.at[:, :, 0], pfar.at[:, 0])):
+            left(part, (pb_s, pb_r), i)
 
     for copy in sent:
         copy.wait_send()
@@ -326,13 +374,13 @@
             pltpu.VMEM((4, B, 256), BF),
             pltpu.VMEM((4, B, 256), BF),
             pltpu.VMEM((1024, 256), BF),
-            pltpu.VMEM((10, B, 256), BF),
-            pltpu.VMEM((2, 10, B, 256), BF),
-            pltpu.VMEM((2, B, 256), BF),
+            pltpu.VMEM((10, 2, B, 256), BF),
+            pltpu.VMEM((2, 10, 2, B, 256), BF),
+            pltpu.VMEM((2, 2, B, 256), BF),
             pltpu.VMEM((16, 5, 128), F32),
             pltpu.VMEM((16, 5, 128), F32),
             dma((9,)),
-        ] + [dma((n,)) for n in (2, 5, 5, 2, 4, 4, 25, 2, 4, 1, 2, 2, 15, 15) for _ in range(2)] + [
+        ] + [dma((n,)) for n in (2, 5, 5, 2, 4, 4, 25, 2, 1, 4, 1, 4, 2, 3, 15, 15) for _ in range(2)] + [
             pltpu.SemaphoreType.REGULAR] + [pltpu.SemaphoreType.REGULAR] * 3,
         compiler_params=pltpu.CompilerParams(
             collective_id=0, has_side_effects=True, vmem_limit_bytes=24 << 20

time: 49.2 us -> 48 us (0.976)
  Pallas kernels: 48.4 us -> 47.2 us
    pallas_call x1, Pallas kernels: 47.2 us -> 46 us  [on_device(): pl.pallas_call(kernel, out_shape=out_shape, in_specs=[hbm] * 6, out_specs...]
where the time goes in v3:
time: 48 us; the launch traced here: 47.9 us
  Pallas kernels  47.2 us (98%)
  between operations  0.64 us (1%)
    pallas_call x1, Pallas kernels, on_device(): pl.pallas_call(kernel, out_shape=out_shape, in_specs=[hbm] * 6, out_specs...  46 us
    pallas_call x1, Pallas kernels, on_device(): pl.pallas_call(hand_over, out_shape=out_shape, in_specs=[anywhere] * 5, o...  1.21 us

profile of v3, /device:TPU:24, one launch (start us, length us, event | category | flops | bytes accessed | tf_op | source)
XLA Modules:
  0.0 47.9 jit_solution(5887658036237571472)
XLA Ops:
  0.6 46.0 %kv_backward_adafactor.1 = (f32[1,1,32,256]{3,2,1,0:T(8,128)S(1)}, f32[1,1,1,32]{3,2,1,0:T(1,128)S(1)}, f32[1,256]{1,0:T(1,128)S(1)}, bf16[1024,256]{1,0:T(8,128)(2,1)S(1)}, bf16[1024,512]{1,0:T(8,128)(2,1)S(1)}) custom-call(bf16[1024,1024]{1,0:T(8,128)(2,1)} %a_hbm.1, bf16[1024,256]{1,0:T(8,128)(2,1)} %kv_hbm.1, bf16[1024,256]{1,0:T(8,128)(2,1)} %w_hbm.1, ...), custom_call_target="tpu_custom_call" | custom-call | tf_op jit(solution)/shard_map/kv_backward_adafactor/pallas_call | solution.py:353
  46.7 1.2 %hand_over.1 = (f32[1,1,32,256]{3,2,1,0:T(8,128)}, f32[1,1,1,32]{3,2,1,0:T(1,128)}, f32[1,256]{1,0:T(1,128)}, bf16[1024,256]{1,0:T(8,128)(2,1)}, bf16[1024,512]{1,0:T(8,128)(2,1)}) custom-call(f32[1,1,32,256]{3,2,1,0:T(8,128)S(1)} %get-tuple-element.10.refs_0_, f32[1,1,1,32]{3,2,1,0:T(1,128)S(1)} %get-tuple-element.11.refs_1_, ...), custom_call_target="tpu_custom_call" | custom-call | tf_op jit(solution)/shard_map/hand_over/pallas_call | solution.py:390

commit v4 on v3

--- a/solution.py
+++ b/solution.py
@@ -331,9 +331,13 @@
 def hand_over(*refs):
     n = len(refs) // 2
     sems = refs[-1]
-    copies = [pltpu.make_async_copy(refs[i], refs[n + i], sems.at[i]) for i in range(n)]
-    for copy in copies:
-        copy.start()
+    copies = []
+    for src, dst in zip(refs[:n], refs[n:-1]):
+        parts = 4 if src.shape[0] == 1024 else 1
+        for i in range(parts):
+            piece = pl.ds(i * (src.shape[0] // parts), src.shape[0] // parts)
+            copies.append(pltpu.make_async_copy(src.at[piece], dst.at[piece], sems.at[len(copies)]))
+            copies[-1].start()
     for copy in copies:
         copy.wait()
 
@@ -392,7 +396,7 @@
         out_shape=out_shape,
         in_specs=[anywhere] * 5,
         out_specs=(hbm,) * 5,
-        scratch_shapes=[dma((5,))],
+        scratch_shapes=[dma((11,))],
         compiler_params=pltpu.CompilerParams(vmem_limit_bytes=16 << 20),
         name="hand_over",
     )(*results)

time: 48 us -> 48 us (level)
  no operation moved by 1% of the time
where the time goes in v4:
time: 48 us; the launch traced here: 47.9 us
  Pallas kernels  47.3 us (99%)
  between operations  0.64 us (1%)
    pallas_call x1, Pallas kernels, on_device(): pl.pallas_call(kernel, out_shape=out_shape, in_specs=[hbm] * 6, out_specs...  46 us
    pallas_call x1, Pallas kernels, on_device(): pl.pallas_call(hand_over, out_shape=out_shape, in_specs=[anywhere] * 5, o...  1.25 us

profile of v4, /device:TPU:24, one launch (start us, length us, event | category | flops | bytes accessed | tf_op | source)
XLA Modules:
  0.0 47.9 jit_solution(3658839434804508713)
XLA Ops:
  0.6 46.0 %kv_backward_adafactor.1 = (f32[1,1,32,256]{3,2,1,0:T(8,128)S(1)}, f32[1,1,1,32]{3,2,1,0:T(1,128)S(1)}, f32[1,256]{1,0:T(1,128)S(1)}, bf16[1024,256]{1,0:T(8,128)(2,1)S(1)}, bf16[1024,512]{1,0:T(8,128)(2,1)S(1)}) custom-call(bf16[1024,1024]{1,0:T(8,128)(2,1)} %a_hbm.1, bf16[1024,256]{1,0:T(8,128)(2,1)} %kv_hbm.1, bf16[1024,256]{1,0:T(8,128)(2,1)} %w_hbm.1, ...), custom_call_target="tpu_custom_call" | custom-call | tf_op jit(solution)/shard_map/kv_backward_adafactor/pallas_call | solution.py:357
  46.7 1.3 %hand_over.1 = (f32[1,1,32,256]{3,2,1,0:T(8,128)}, f32[1,1,1,32]{3,2,1,0:T(1,128)}, f32[1,256]{1,0:T(1,128)}, bf16[1024,256]{1,0:T(8,128)(2,1)}, bf16[1024,512]{1,0:T(8,128)(2,1)}) custom-call(f32[1,1,32,256]{3,2,1,0:T(8,128)S(1)} %get-tuple-element.10.refs_0_, f32[1,1,1,32]{3,2,1,0:T(1,128)S(1)} %get-tuple-element.11.refs_1_, ...), custom_call_target="tpu_custom_call" | custom-call | tf_op jit(solution)/shard_map/hand_over/pallas_call | solution.py:394

commit v5 on v3

--- a/solution.py
+++ b/solution.py
@@ -142,8 +142,6 @@
     half = w_v.shape[0] // 2
     mine = pl.ds(pl.multiple_of(core * half, half), half)
     theirs = pl.ds(pl.multiple_of((1 - core) * half, half), half)
-    send(kv, kvo, (core_s, core_r), 0, dev(dc=1))
-    send(w_v.at[theirs], wo, (core_s, core_r), 1, dev(dc=1))
 
     def aggregate(j):
         a = AGG[j]
@@ -165,6 +163,8 @@
         arrived(f_in.at[n], (f_s, f_r), n)
     aggregate(0)
     aggregate(1)
+    send(kv, kvo, (core_s, core_r), 0, dev(dc=1))
+    send(w_v.at[theirs], wo, (core_s, core_r), 1, dev(dc=1))
     for n in range(5):
         arrived(n_in.at[n], (n_s, n_r), n)
     aggregate(2)

time: 48 us -> 48 us (level)
  no operation moved by 1% of the time
where the time goes in v5:
time: 48 us; the launch traced here: 47.9 us
  Pallas kernels  47.2 us (98%)
  between operations  0.64 us (1%)
    pallas_call x1, Pallas kernels, on_device(): pl.pallas_call(kernel, out_shape=out_shape, in_specs=[hbm] * 6, out_specs...  46 us
    pallas_call x1, Pallas kernels, on_device(): pl.pallas_call(hand_over, out_shape=out_shape, in_specs=[anywhere] * 5, o...  1.21 us

profile of v5, /device:TPU:24, one launch (start us, length us, event | category | flops | bytes accessed | tf_op | source)
XLA Modules:
  0.0 47.9 jit_solution(14096306685999163087)
XLA Ops:
  0.6 46.0 %kv_backward_adafactor.1 = (f32[1,1,32,256]{3,2,1,0:T(8,128)S(1)}, f32[1,1,1,32]{3,2,1,0:T(1,128)S(1)}, f32[1,256]{1,0:T(1,128)S(1)}, bf16[1024,256]{1,0:T(8,128)(2,1)S(1)}, bf16[1024,512]{1,0:T(8,128)(2,1)S(1)}) custom-call(bf16[1024,1024]{1,0:T(8,128)(2,1)} %a_hbm.1, bf16[1024,256]{1,0:T(8,128)(2,1)} %kv_hbm.1, bf16[1024,256]{1,0:T(8,128)(2,1)} %w_hbm.1, ...), custom_call_target="tpu_custom_call" | custom-call | tf_op jit(solution)/shard_map/kv_backward_adafactor/pallas_call | solution.py:353
  46.7 1.2 %hand_over.1 = (f32[1,1,32,256]{3,2,1,0:T(8,128)}, f32[1,1,1,32]{3,2,1,0:T(1,128)}, f32[1,256]{1,0:T(1,128)}, bf16[1024,256]{1,0:T(8,128)(2,1)}, bf16[1024,512]{1,0:T(8,128)(2,1)}) custom-call(f32[1,1,32,256]{3,2,1,0:T(8,128)S(1)} %get-tuple-element.10.refs_0_, f32[1,1,1,32]{3,2,1,0:T(1,128)S(1)} %get-tuple-element.11.refs_1_, ...), custom_call_target="tpu_custom_call" | custom-call | tf_op jit(solution)/shard_map/hand_over/pallas_call | solution.py:390
